TPU v7x, 128 devices: a whole 4x4x4 slice. The times are simulated.
128 devices in a mesh: rep: 4 (over z_lo, core), fsdp: 32 (over y, x, z_hi).
Axes of the slice: x: 4, y: 4, z: 4 (z_hi: 2, z_lo: 2; z = z_hi * 2 + z_lo), core: 2. Of those that a mesh axis runs over, the one named last changes fastest.
Arguments:
- activations: bfloat16 [4, 16384, 6144], P('rep', 'fsdp'), may hold values from -6 to 6
- cotangent: bfloat16 [4, 16384, 1024], P('rep', 'fsdp'), may hold values from -0.125 to 0.125
- weight: bfloat16 [4, 6144, 1024], P('rep', 'fsdp'), may hold values from -6 to 6
- first_moment: bfloat16 [4, 6144, 1024], P('rep', 'fsdp'), may hold values from -12 to 12
- second_moment: bfloat16 [4, 6144, 1024], P('rep', 'fsdp'), may hold values from 1 to 16
- anchor: bfloat16 [6144, 1024], P('fsdp'), may hold values from -6 to 6
- momentum: float32 [6144, 1024], P('fsdp'), may hold values from -6 to 6
- exponents: int32 [6144, 8], P('fsdp'), may hold values from -2 to 1
Outputs:
- new_weight: bfloat16 [4, 6144, 1024], P('rep', 'fsdp')
- new_first: bfloat16 [4, 6144, 1024], P('rep', 'fsdp')
- new_second: bfloat16 [4, 6144, 1024], P('rep', 'fsdp')
- new_anchor: bfloat16 [6144, 1024], P('fsdp')
- new_momentum: float32 [6144, 1024], P('fsdp')
Inputs may be any that keep to these rules, and one draw needn't show every extreme that they name: `exponents`: one exponent for each block of 128 consecutive columns of a row.
All inputs are finite; a program needn't handle non-finite values.
Results may differ from a plain program's by a relative error of at most 0.02.
Values may be sent and summed in bfloat16 or wider, within the bound.
A program may use at most 128 MiB of HBM per device.

v0:
```python
import jax
import jax.numpy as jnp
from jax import lax
from jax.sharding import PartitionSpec as P


def local(activations, cotangent, weight, first_moment, second_moment, anchor, momentum, exponents):
    tok_rows = activations[0]
    cot_rows = cotangent[0]
    own_rows = anchor.shape[0]
    width = anchor.shape[1]
    grad = lax.psum_scatter(
        lax.dot_general(
            tok_rows, cot_rows, (((0,), (0,)), ((), ())), preferred_element_type=jnp.float32
        ).astype(jnp.bfloat16),
        "fsdp",
        scatter_dimension=0,
        tiled=True,
    ).astype(jnp.float32)
    first = (0.9 * first_moment[0].astype(jnp.float32) + 0.1 * grad).astype(jnp.bfloat16)
    second = (0.95 * second_moment[0].astype(jnp.float32) + 0.05 * grad * grad).astype(jnp.bfloat16)
    old = weight[0].astype(jnp.float32)
    update = first.astype(jnp.float32) / (jnp.sqrt(second.astype(jnp.float32)) + 1e-08)
    fresh = (old - 0.1 * (update + 0.01 * old)).astype(jnp.bfloat16)
    power = exponents.astype(jnp.float32)[:, :, None]
    blocks = exponents.shape[1]
    anchor_f = anchor.astype(jnp.float32)
    gap = (anchor_f - fresh.astype(jnp.float32)).reshape(own_rows, blocks, 128)
    packed = (
        jnp.clip(gap * jnp.exp2(-power), -4.0, 4.0).reshape(own_rows, width).astype(jnp.bfloat16)
    )
    replicas = lax.axis_size("rep")
    total = lax.psum(packed.astype(jnp.float32).astype(jnp.bfloat16), "rep").astype(jnp.float32)
    outer = (jnp.exp2(power) * total.reshape(own_rows, blocks, 128)).reshape(
        own_rows, width
    ) / replicas
    new_momentum = 0.9 * momentum + outer
    new_anchor = (anchor_f - 0.7 * (outer + 0.9 * new_momentum)).astype(jnp.bfloat16)
    return (fresh[None], first[None], second[None], new_anchor, new_momentum)


def solution(mesh):
    return jax.shard_map(
        local,
        mesh=mesh,
        in_specs=(
            P("rep", "fsdp", None),
            P("rep", "fsdp", None),
            P("rep", "fsdp", None),
            P("rep", "fsdp", None),
            P("rep", "fsdp", None),
            P("fsdp", None),
            P("fsdp", None),
            P("fsdp", None),
        ),
        out_specs=(
            P("rep", "fsdp", None),
            P("rep", "fsdp", None),
            P("rep", "fsdp", None),
            P("fsdp", None),
            P("fsdp", None),
        ),
        check_vma=False,
    )
```

profile of v0, /device:TPU:1, one launch (start us, length us, event | category | flops | bytes accessed | tf_op | source)
XLA Modules:
  0.0 323.8 jit_solution(17780872109913706294)
XLA Ops:
  7.2 0.0 copy-start
  7.2 0.0 reduce-scatter.2.cloned.1.call-start
  7.2 1.2 copy-done
  8.4 12.6 %convolution_convert_fusion = bf16[6144,1024]{1,0:T(8,128)(2,1)} fusion(bf16[1,512,6144]{2,1,0:T(8,128)(2,1)} %param.8, bf16[1,512,1024]{2,1,0:T(8,128)(2,1)S(1)} %copy-done), kind=kOutput, calls=%fused_computation | convolution fusion | flops 6448742400 | bytes 19922944 | tf_op jit(solution)/shard_map/dot_general | solution.py:13
  21.0 0.0 copy-start.6
  21.0 0.0 copy-start.1
  21.0 0.0 copy-start.3
  21.0 0.0 copy-start.4
  21.0 0.0 copy-start.5
  21.0 0.0 reduce-scatter.2.cloned.1.call-update
  21.0 0.0 copy-start.2
  21.0 0.0 all-reduce.2.cloned.1.call-start
  21.1 0.6 copy-done.6
  21.7 0.1 copy.14
  21.8 252.9 %reduce-scatter.2.cloned.1.call-done = bf16[192,1024]{1,0:T(8,128)(2,1)} async-done(((bf16[6144,1024]{1,0:T(8,128)(2,1)}), bf16[192,1024]{1,0:T(8,128)(2,1)}) %reduce-scatter.2.cloned.1.call-update) | async-done | bytes 393232 | tf_op jit(solution)/shard_map/reduce_scatter | solution.py:12
  274.6 0.3 mul.84
  274.9 0.0 copy-done.1
  274.9 0.0 copy-done.3
  274.9 0.0 copy-done.4
  274.9 0.0 copy-done.5
  274.9 3.0 fusion.6
  278.0 0.0 all-reduce.2.cloned.1.call-update
  278.0 0.1 copy.13
  278.1 36.3 %all-reduce.2.cloned.1.call-done = bf16[192,1024]{1,0:T(8,128)(2,1)} async-done(((bf16[192,1024]{1,0:T(8,128)(2,1)}), bf16[192,1024]{1,0:T(8,128)(2,1)}) %all-reduce.2.cloned.1.call-update) | async-done | bytes 393232 | tf_op jit(solution)/shard_map/psum | solution.py:33
  314.3 0.3 mul.82
  314.6 0.0 copy-done.2
  314.6 2.4 fusion.7
  (1 shorter events, 0.0 us)
Async XLA Ops:
  7.2 1.2 copy-start
  7.2 267.5 %reduce-scatter.2.cloned.1.call-start = ((), (), s32[]{:S(2)}) async-start(), calls=%async_computation.1 | async-start | bytes 12976128 | tf_op jit(solution)/shard_map/reduce_scatter | solution.py:12
  21.0 0.7 copy-start.6
  21.0 253.9 %copy-start.1 = (bf16[192,1024]{1,0:T(8,128)(2,1)S(1)}, bf16[192,1024]{1,0:T(8,128)(2,1)}, u32[]{:S(2)}) copy-start(bf16[192,1024]{1,0:T(8,128)(2,1)} %param.13) | copy-start | bytes 1179652
  21.0 253.9 %copy-start.3 = (bf16[1,192,1024]{2,1,0:T(8,128)(2,1)S(1)}, bf16[1,192,1024]{2,1,0:T(8,128)(2,1)}, u32[]{:S(2)}) copy-start(bf16[1,192,1024]{2,1,0:T(8,128)(2,1)} %param.12) | copy-start | bytes 1179652
  21.0 254.0 %copy-start.4 = (bf16[1,192,1024]{2,1,0:T(8,128)(2,1)S(1)}, bf16[1,192,1024]{2,1,0:T(8,128)(2,1)}, u32[]{:S(2)}) copy-start(bf16[1,192,1024]{2,1,0:T(8,128)(2,1)} %param.11) | copy-start | bytes 1179652
  21.0 254.0 %copy-start.5 = (bf16[1,192,1024]{2,1,0:T(8,128)(2,1)S(1)}, bf16[1,192,1024]{2,1,0:T(8,128)(2,1)}, u32[]{:S(2)}) copy-start(bf16[1,192,1024]{2,1,0:T(8,128)(2,1)} %param.10) | copy-start | bytes 1179652
  21.0 293.6 %copy-start.2 = (f32[192,1024]{1,0:T(8,128)S(1)}, f32[192,1024]{1,0:T(8,128)}, u32[]{:S(2)}) copy-start(f32[192,1024]{1,0:T(8,128)} %param.14) | copy-start | bytes 2359300
  21.0 293.3 %all-reduce.2.cloned.1.call-start = ((), (), s32[]{:S(2)}) async-start(), calls=%async_computation.2 | async-start | bytes 786432 | tf_op jit(solution)/shard_map/psum | solution.py:33
Sparse Core Ops, SparseCore 0:
  21.1 253.4 reduce-scatter.1
  278.1 36.2 all-reduce.1
where the time goes:
time: 324 us
  waiting for transfers between devices  289 us (89%)
  between operations  14.1 us (4%)
  matrix products  12.6 us (4%)
  other arithmetic  5.39 us (2%)
    reduce_scatter x1, waiting for transfers between devices, local(): lax.psum_scatter(lax.dot_general(tok_rows, cot_rows, (((0,), (0,)), ((),...  253 us
    psum x1, waiting for transfers between devices, local(): lax.psum(packed.astype(jnp.float32).astype(jnp.bfloat16), 'rep')  36.3 us
    dot_general x1, matrix products, local(): lax.dot_general(tok_rows, cot_rows, (((0,), (0,)), ((), ())), preferred_e...  12.6 us
  transfers between devices with their start and end apart: 2, of which 2 were waited for; matrix products, arithmetic and copies ran while one was open for 0% of the time, Pallas kernels for 0%

commit v1 on v0

v1 whole, which is shorter than its diff:
```python
import jax
import jax.numpy as jnp
from jax import lax
from jax.experimental import pallas as pl
from jax.experimental.pallas import tpu as pltpu
from jax.sharding import PartitionSpec as P

MESH = pl.DeviceIdType.MESH
BF = jnp.bfloat16
F32 = jnp.float32

RING = 4
REPS = 4
GW = 256
OFFS = (2, 1, 3, 0)
A_SLOT = (0, 4, 2, 6)
B_SLOT = (3, 1, 5, 7)
NEW_BLOCKS = (
    ((0, 0), (0, 1), (0, 2), (1, 0), (2, 0)),
    ((1, 1), (1, 2), (2, 1)),
    ((2, 2), (0, 3), (3, 0)),
    ((3, 1), (3, 2), (1, 3), (2, 3), (3, 3)),
)


def plus(*terms):
    total = terms[0].astype(F32)
    for term in terms[1:]:
        total = total + term.astype(F32)
    return total


def kernel(act, cot, weight, first_in, second_in, anchor_in, mom_in, exps,
           w_out, f_out, s_out, anc_out, mom_out,
           a_v, c_v, w_v, f_v, s_v, anc_v, mom_v,
           part, rp, rm, fp, fm, part2, rp2, rm2, fp2, fm2, wsum, rz, packs,
           wo_v, fo_v, so_v, ao_v, mo_v,
           a_sem, c_sem, in_sem, out_sem,
           sp_s, sp_r, sm_s, sm_r, fp_s, fp_r, fm_s, fm_r,
           sp2_s, sp2_r, sm2_s, sm2_r, fp2_s, fp2_r, fm2_s, fm2_r,
           z_s, z_r, k_s, k_r):
    groups = c_v.shape[1] // GW
    own = w_v.shape[0]
    half = own // 2
    block = 2 * own
    rep = lax.axis_index("rep")
    f = lax.axis_index("fsdp")
    zlo, core = rep // 2, rep % 2
    zhi, x, y = f % 2, (f // 2) % RING, f // (2 * RING)

    def dev(x=x, y=y, zhi=zhi, rep=rep):
        return (rep, (y * RING + x) * 2 + zhi)

    xp, xm = dev(x=(x + 1) % RING), dev(x=(x + RING - 1) % RING)
    yp, ym = dev(y=(y + 1) % RING), dev(y=(y + RING - 1) % RING)
    zdev = dev(zhi=1 - zhi)
    mates = [dev(rep=(rep + i) % REPS) for i in range(1, REPS)]
    up1, down1 = (xp, yp), (xm, ym)
    up2, down2 = (yp, xp), (ym, xm)

    def cols(g):
        return pl.ds(pl.multiple_of(g * GW, GW), GW)

    def a_copy(blk):
        at = pl.ds(pl.multiple_of(blk * block, block), block)
        return pltpu.make_async_copy(act.at[0, :, at], a_v.at[:, at], a_sem.at[blk])

    def c_copy(g):
        return pltpu.make_async_copy(cot.at[0, :, cols(g)], c_v.at[:, cols(g)], c_sem.at[g])

    ins = [
        pltpu.make_async_copy(src, dst, in_sem.at[i])
        for i, (src, dst) in enumerate((
            (weight.at[0], w_v), (first_in.at[0], f_v), (second_in.at[0], s_v), (anchor_in, anc_v), (mom_in, mom_v)))
    ]

    def inner_outs(g):
        return [
            pltpu.make_async_copy(src.at[:, cols(g)], dst.at[0, :, cols(g)], out_sem.at[i, g])
            for i, (src, dst) in enumerate(((wo_v, w_out), (fo_v, f_out), (so_v, s_out)))
        ]

    def outer_outs(g):
        return [
            pltpu.make_async_copy(src.at[:, cols(g)], dst.at[:, cols(g)], out_sem.at[3 + i, g])
            for i, (src, dst) in enumerate(((ao_v, anc_out), (mo_v, mom_out)))
        ]

    def remote(src, dst, s, r, to):
        return pltpu.make_async_remote_copy(
            src_ref=src, dst_ref=dst, send_sem=s, recv_sem=r, device_id=to, device_id_type=MESH)

    def c_sp(h, g, k):
        return remote(part.at[h, g, k, pl.ds(0, 2)], rp.at[h, g, k], sp_s.at[h, g, k], sp_r.at[h, g, k], up1[h])

    def c_sm(h, g, k):
        return remote(part.at[h, g, k, pl.ds(2, 2)], rm.at[h, g, k], sm_s.at[h, g, k], sm_r.at[h, g, k], down1[h])

    def c_fp(h, g, k):
        return remote(rp.at[h, g, k, 0], fp.at[h, g, k], fp_s.at[h, g, k], fp_r.at[h, g, k], up1[h])

    def c_fm(h, g, k):
        return remote(rm.at[h, g, k, 1], fm.at[h, g, k], fm_s.at[h, g, k], fm_r.at[h, g, k], down1[h])

    def c_sp2(h, g):
        return remote(part2.at[h, g, pl.ds(0, 2)], rp2.at[h, g], sp2_s.at[h, g], sp2_r.at[h, g], up2[h])

    def c_sm2(h, g):
        return remote(part2.at[h, g, pl.ds(2, 2)], rm2.at[h, g], sm2_s.at[h, g], sm2_r.at[h, g], down2[h])

    def c_fp2(h, g):
        return remote(rp2.at[h, g, 0], fp2.at[h, g], fp2_s.at[h, g], fp2_r.at[h, g], up2[h])

    def c_fm2(h, g):
        return remote(rm2.at[h, g, 1], fm2.at[h, g], fm2_s.at[h, g], fm2_r.at[h, g], down2[h])

    def c_z(g):
        return remote(wsum.at[1 - zhi, g], rz.at[g], z_s.at[g], z_r.at[g], zdev)

    def c_pack(g, i):
        return remote(packs.at[g, rep], packs.at[g, rep], k_s.at[g, i], k_r.at[g, i], mates[i])

    def products(g, k):
        @pl.when(g == 0)
        def _():
            for ry, rx in NEW_BLOCKS[k]:
                a_copy(((y + OFFS[ry]) % RING) * RING + (x + OFFS[rx]) % RING).wait()

        if k == 0:
            c_copy(g).wait()
        right = c_v[:, cols(g)]
        for ry, rx in NEW_BLOCKS[k]:
            blk = ((y + OFFS[ry]) % RING) * RING + (x + OFFS[rx]) % RING
            at = pl.ds(pl.multiple_of(blk * block, block), block)
            tile = lax.dot_general(
                a_v[:, at], right, (((0,), (0,)), ((), ())), preferred_element_type=F32).astype(BF)
            part[0, g, ry, A_SLOT[rx]] = tile[:half]
            part[0, g, ry, B_SLOT[rx]] = tile[half:own]
            part[1, g, rx, A_SLOT[ry]] = tile[own:own + half]
            part[1, g, rx, B_SLOT[ry]] = tile[own + half:]
        for h in range(2):
            c_sp(h, g, k).start()
            c_sm(h, g, k).start()

    def forward(g, k):
        for h in range(2):
            c_sp(h, g, k).wait_recv()
            rp[h, g, k, 0] = plus(rp[h, g, k, 0], part[h, g, k, 4]).astype(BF)
            c_fp(h, g, k).start()
            c_sm(h, g, k).wait_recv()
            rm[h, g, k, 1] = plus(rm[h, g, k, 1], part[h, g, k, 5]).astype(BF)
            c_fm(h, g, k).start()

    def first_sum(g, k):
        for h in range(2):
            c_fp(h, g, k).wait_recv()
            c_fm(h, g, k).wait_recv()
            part2[h, g, A_SLOT[k]] = plus(part[h, g, k, 6], fp[h, g, k], rm[h, g, k, 0]).astype(BF)
            part2[h, g, B_SLOT[k]] = plus(part[h, g, k, 7], fm[h, g, k], rp[h, g, k, 1]).astype(BF)
            if k == 2:
                c_sp2(h, g).start()
                c_sm2(h, g).start()

    def forward2(g):
        for h in range(2):
            c_sp2(h, g).wait_recv()
            rp2[h, g, 0] = plus(rp2[h, g, 0], part2[h, g, 4]).astype(BF)
            c_fp2(h, g).start()
            c_sm2(h, g).wait_recv()
            rm2[h, g, 1] = plus(rm2[h, g, 1], part2[h, g, 5]).astype(BF)
            c_fm2(h, g).start()

    def second_sum(g):
        for h in range(2):
            c_fp2(h, g).wait_recv()
            c_fm2(h, g).wait_recv()
            wsum[h, g, pl.ds(0, half)] = plus(part2[h, g, 6], fp2[h, g], rm2[h, g, 0]).astype(BF)
            wsum[h, g, pl.ds(half, half)] = plus(part2[h, g, 7], fm2[h, g], rp2[h, g, 1]).astype(BF)
        c_z(g).start()

    def powers(g):
        lane = lax.broadcasted_iota(jnp.int32, exps.shape, 1)
        per = GW // 128
        parts = []
        for i in range(per):
            one = jnp.sum(jnp.where(lane == g * per + i, exps[...].astype(F32), 0.0), axis=1, keepdims=True)
            parts.append(jnp.broadcast_to(one, (own, 128)))
        return jnp.concatenate(parts, axis=1)

    def inner(g):
        c_z(g).wait_recv()
        @pl.when(g == 0)
        def _():
            for copy in ins:
                copy.wait()
        at = cols(g)
        grad = plus(wsum[zhi, g], rz[g])
        first = (0.9 * f_v[:, at].astype(F32) + 0.1 * grad).astype(BF)
        second = (0.95 * s_v[:, at].astype(F32) + 0.05 * grad * grad).astype(BF)
        old = w_v[:, at].astype(F32)
        update = first.astype(F32) / (jnp.sqrt(second.astype(F32)) + 1e-08)
        fresh = (old - 0.1 * (update + 0.01 * old)).astype(BF)
        fo_v[:, at] = first
        so_v[:, at] = second
        wo_v[:, at] = fresh
        gap = anc_v[:, at].astype(F32) - fresh.astype(F32)
        packs[g, rep] = jnp.clip(gap * jnp.exp2(-powers(g)), -4.0, 4.0).astype(BF)
        for i in range(REPS - 1):
            c_pack(g, i).start()
        for copy in inner_outs(g):
            copy.start()

    def outer(g):
        for i in range(REPS - 1):
            c_pack(g, i).wait_recv()
        at = cols(g)
        total = plus(*[packs[g, i] for i in range(REPS)])
        step = (jnp.exp2(powers(g)) * total) / REPS
        momentum = 0.9 * mom_v[:, at] + step
        mo_v[:, at] = momentum
        ao_v[:, at] = (anc_v[:, at].astype(F32) - 0.7 * (step + 0.9 * momentum)).astype(BF)
        for copy in outer_outs(g):
            copy.start()

    c_copy(0).start()
    for k in range(4):
        for ry, rx in NEW_BLOCKS[k]:
            a_copy(((y + OFFS[ry]) % RING) * RING + (x + OFFS[rx]) % RING).start()
    for g in range(1, groups):
        c_copy(g).start()
    for copy in ins:
        copy.start()

    everyone = [xp, xm, yp, ym, zdev] + mates
    barrier = pltpu.get_barrier_semaphore()
    for to in everyone:
        pl.semaphore_signal(barrier, inc=1, device_id=to, device_id_type=MESH)
    pl.semaphore_wait(barrier, len(everyone))

    @pl.loop(0, groups + 2)
    def _(turn):
        g = turn - 1
        for k in range(4):
            ahead, k2 = g + (k + 2) // 4, (k + 2) % 4
            nxt, k1 = g + (k + 1) // 4, (k + 1) % 4

            @pl.when(jnp.logical_and(ahead >= 0, ahead < groups))
            def _():
                products(ahead, k2)

            @pl.when(jnp.logical_and(nxt >= 0, nxt < groups))
            def _():
                forward(nxt, k1)

            @pl.when(jnp.logical_and(g >= 0, g < groups))
            def _():
                first_sum(g, k)
                if k == 3:
                    forward2(g)

            if k < 3:
                @pl.when(g >= 1)
                def _():
                    (second_sum, inner, outer)[k](g - 1)

    @pl.loop(0, groups)
    def _(g):
        for h in range(2):
            for k in range(4):
                c_sp(h, g, k).wait_send()
                c_sm(h, g, k).wait_send()
                c_fp(h, g, k).wait_send()
                c_fm(h, g, k).wait_send()
            c_sp2(h, g).wait_send()
            c_sm2(h, g).wait_send()
            c_fp2(h, g).wait_send()
            c_fm2(h, g).wait_send()
        c_z(g).wait_send()
        for i in range(REPS - 1):
            c_pack(g, i).wait_send()
        for copy in inner_outs(g) + outer_outs(g):
            copy.wait()


def local(activations, cotangent, weight, first_moment, second_moment, anchor, momentum, exponents):
    own, width = anchor.shape
    tokens, rows = activations.shape[1:]
    groups = width // GW
    half = own // 2
    dma = pltpu.SemaphoreType.DMA
    anywhere = pl.BlockSpec(memory_space=pl.ANY)

    def buf(*shape, kind=BF):
        return pltpu.VMEM(shape, kind)

    return pl.pallas_call(
        kernel,
        out_shape=(
            jax.ShapeDtypeStruct(weight.shape, BF),
            jax.ShapeDtypeStruct(weight.shape, BF),
            jax.ShapeDtypeStruct(weight.shape, BF),
            jax.ShapeDtypeStruct(anchor.shape, BF),
            jax.ShapeDtypeStruct(momentum.shape, F32),
        ),
        in_specs=[anywhere] * 7 + [pl.BlockSpec(memory_space=pltpu.VMEM)],
        out_specs=[anywhere] * 5,
        scratch_shapes=[
            buf(tokens, rows), buf(tokens, width),
            buf(own, width), buf(own, width), buf(own, width), buf(own, width), buf(own, width, kind=F32),
            buf(2, groups, 4, 8, half, GW),
            buf(2, groups, 4, 2, half, GW), buf(2, groups, 4, 2, half, GW),
            buf(2, groups, 4, half, GW), buf(2, groups, 4, half, GW),
            buf(2, groups, 8, half, GW),
            buf(2, groups, 2, half, GW), buf(2, groups, 2, half, GW),
            buf(2, groups, half, GW), buf(2, groups, half, GW),
            buf(2, groups, own, GW), buf(groups, own, GW), buf(groups, REPS, own, GW),
            buf(own, width), buf(own, width), buf(own, width), buf(own, width), buf(own, width, kind=F32),
            dma((RING * RING,)), dma((groups,)), dma((5,)), dma((5, groups)),
        ] + [dma((2, groups, 4))] * 8 + [dma((2, groups))] * 8
        + [dma((groups,))] * 2 + [dma((groups, REPS - 1))] * 2,
        compiler_params=pltpu.CompilerParams(
            collective_id=0, has_side_effects=True, vmem_limit_bytes=58 * 1024 * 1024),
        cost_estimate=pl.CostEstimate(
            flops=2 * tokens * rows * width, bytes_accessed=12 * 2 ** 20, transcendentals=0),
        name="diloco_step",
    )(activations, cotangent, weight, first_moment, second_moment, anchor, momentum, exponents)


def solution(mesh):
    split = P("rep", "fsdp", None)
    rows = P("fsdp", None)
    return jax.shard_map(
        local,
        mesh=mesh,
        in_specs=(split, split, split, split, split, rows, rows, rows),
        out_specs=(split, split, split, rows, rows),
        check_vma=False,
    )
```

time: 324 us -> 111 us (0.34)
  waiting for transfers between devices: 289 us -> 0 us
  Pallas kernels: 0 us -> 99.6 us
  between operations: 14.1 us -> 0.64 us
  matrix products: 12.6 us -> 0 us
  local copies, waits for them, and re-layouts: 2.52 us -> 10.6 us
  other arithmetic: 5.39 us -> 0 us
    reduce_scatter x1 -> x0, waiting for transfers between devices: 253 us -> none  [local(): lax.psum_scatter(lax.dot_general(tok_rows, cot_rows, (((0,), (0,)), ((),...]
    pallas_call x0 -> x1, Pallas kernels: none -> 99.6 us  [local(): pl.pallas_call(kernel, out_shape=(jax.ShapeDtypeStruct(weight.shape, BF),...]
    psum x1 -> x0, waiting for transfers between devices: 36.3 us -> none  [local(): lax.psum(packed.astype(jnp.float32).astype(jnp.bfloat16), 'rep')]
    dot_general x1 -> x0, matrix products: 12.6 us -> none  [local(): lax.dot_general(tok_rows, cot_rows, (((0,), (0,)), ((), ())), preferred_e...]
    unnamed x14 -> x6, local copies, waits for them, and re-layouts: 1.79 us -> 10.6 us
    convert_element_type x2 -> x0, other arithmetic: 5.38 us -> none  [the longest x1 3.01 us: local(): jnp.clip(gap * jnp.exp2(-power), -4.0, 4.0).reshape(own_rows, width)]
  transfers between devices with their start and end apart: 2 -> 0, of which waited for: 2 -> 0; matrix products, arithmetic and copies ran while one was open for 0% -> 0% of each run, Pallas kernels for 0% -> 0%
where the time goes in v1:
time: 111 us
  Pallas kernels  99.6 us (90%)
  local copies, waits for them, and re-layouts  10.6 us (10%)
    pallas_call x1, Pallas kernels, local(): pl.pallas_call(kernel, out_shape=(jax.ShapeDtypeStruct(weight.shape, BF),...  99.6 us
    unnamed x6, local copies, waits for them, and re-layouts  10.6 us

profile of v1, /device:TPU:1, one launch (start us, length us, event | category | flops | bytes accessed | tf_op | source)
XLA Modules:
  0.0 110.9 jit_solution(13715675792621245002)
XLA Ops:
  0.6 1.5 %copy.13.exps = s32[192,8]{1,0:T(8,128)} copy(s32[192,8]{0,1:T(8,128)} %param.15) | data formatting | bytes 12288 | tf_op args[7]
  2.1 99.6 %diloco_step.1 = (bf16[1,192,1024]{2,1,0:T(8,128)(2,1)}, bf16[1,192,1024]{2,1,0:T(8,128)(2,1)}, bf16[1,192,1024]{2,1,0:T(8,128)(2,1)}, bf16[192,1024]{1,0:T(8,128)(2,1)}, f32[192,1024]{1,0:T(8,128)}) custom-call(bf16[1,512,6144]{2,1,0:T(8,128)(2,1)} %act.1, bf16[1,512,1024]{2,1,0:T(8,128)(2,1)} %cot.1, bf16[1,192,1024]{2,1,0:T(8,128)(2,1)} %weight.1, ...), custom_call_target="tpu_custom_call" | custom-call | flops 6442450944 | bytes 12582912 | tf_op jit(solution)/shard_map/diloco_step/pallas_call | solution.py:296
  101.7 1.8 %copy.19 = bf16[1,192,1024]{2,1,0:T(8,128)(2,1)} copy(bf16[1,192,1024]{2,1,0:T(8,128)(2,1)} %get-tuple-element.10) | data formatting | bytes 786432
  103.5 1.8 %copy.20 = bf16[1,192,1024]{2,1,0:T(8,128)(2,1)} copy(bf16[1,192,1024]{2,1,0:T(8,128)(2,1)} %get-tuple-element.11) | data formatting | bytes 786432
  105.3 1.8 %copy.21 = bf16[1,192,1024]{2,1,0:T(8,128)(2,1)} copy(bf16[1,192,1024]{2,1,0:T(8,128)(2,1)} %get-tuple-element.12) | data formatting | bytes 786432
  107.0 1.8 %copy.22 = bf16[192,1024]{1,0:T(8,128)(2,1)} copy(bf16[192,1024]{1,0:T(8,128)(2,1)} %get-tuple-element.13) | data formatting | bytes 786432
  108.8 2.1 %copy.23 = f32[192,1024]{1,0:T(8,128)} copy(f32[192,1024]{1,0:T(8,128)} %get-tuple-element.14) | data formatting | bytes 1572864

commit v2 on v1

v2 whole, which is shorter than its diff:
```python
import jax
import jax.numpy as jnp
from jax import lax
from jax.experimental import pallas as pl
from jax.experimental.pallas import tpu as pltpu
from jax.sharding import PartitionSpec as P

MESH = pl.DeviceIdType.MESH
BF = jnp.bfloat16
F32 = jnp.float32

RING = 4
REPS = 4
GW = 256
LEAD = 4
FLEAD = 2
LAGS = (1,3,5,7)
OFFS = (2, 1, 3, 0)
A_SLOT = (0, 4, 2, 6)
B_SLOT = (3, 1, 5, 7)
NEW_BLOCKS = (
    ((0, 0), (0, 1), (0, 2), (1, 0), (2, 0)),
    ((1, 1), (1, 2), (2, 1)),
    ((2, 2), (0, 3), (3, 0)),
    ((3, 1), (3, 2), (1, 3), (2, 3), (3, 3)),
)


def plus(*terms):
    total = terms[0].astype(F32)
    for term in terms[1:]:
        total = total + term.astype(F32)
    return total


class Rings:
    def __init__(self, refs, up, down, remote):
        (self.part, self.rp, self.rm, self.fp, self.fm, self.part2, self.rp2, self.rm2, self.fp2, self.fm2) = refs[:10]
        self.sems = refs[10:]
        self.up, self.down, self.remote = up, down, remote
        self.unit = self.part.shape[-2]

    def copy(self, which, h, g, k):
        part, sems = self.part, self.sems
        if which < 4:
            at, up, down = (h, g, k), self.up[h], self.down[h]
            rp, rm, fp, fm = self.rp, self.rm, self.fp, self.fm
        else:
            part, at, up, down = self.part2, (h, g), self.up[1 - h], self.down[1 - h]
            rp, rm, fp, fm = self.rp2, self.rm2, self.fp2, self.fm2
        src, dst, to = (
            (part.at[(*at, pl.ds(0, 2))], rp.at[at], up),
            (part.at[(*at, pl.ds(2, 2))], rm.at[at], down),
            (rp.at[(*at, 0)], fp.at[at], up),
            (rm.at[(*at, 1)], fm.at[at], down),
        )[which % 4]
        return self.remote(src, dst, sems[2 * which].at[at], sems[2 * which + 1].at[at], to)

    def place(self, g, ry, rx, tile):
        u = self.unit
        self.part[0, g, ry, A_SLOT[rx]] = tile[:u]
        self.part[0, g, ry, B_SLOT[rx]] = tile[u:2 * u]
        self.part[1, g, rx, A_SLOT[ry]] = tile[2 * u:3 * u]
        self.part[1, g, rx, B_SLOT[ry]] = tile[3 * u:]

    def send(self, g, k):
        for h in range(2):
            self.copy(0, h, g, k).start()
            self.copy(1, h, g, k).start()

    def forward(self, g, k):
        for h in range(2):
            self.copy(0, h, g, k).wait_recv()
            self.rp[h, g, k, 0] = plus(self.rp[h, g, k, 0], self.part[h, g, k, 4]).astype(BF)
            self.copy(2, h, g, k).start()
            self.copy(1, h, g, k).wait_recv()
            self.rm[h, g, k, 1] = plus(self.rm[h, g, k, 1], self.part[h, g, k, 5]).astype(BF)
            self.copy(3, h, g, k).start()

    def first_sum(self, g, k):
        for h in range(2):
            self.copy(2, h, g, k).wait_recv()
            self.copy(3, h, g, k).wait_recv()
            self.part2[h, g, A_SLOT[k]] = plus(
                self.part[h, g, k, 6], self.fp[h, g, k], self.rm[h, g, k, 0]).astype(BF)
            self.part2[h, g, B_SLOT[k]] = plus(
                self.part[h, g, k, 7], self.fm[h, g, k], self.rp[h, g, k, 1]).astype(BF)
            if k == 2:
                self.copy(4, h, g, 0).start()
                self.copy(5, h, g, 0).start()

    def forward2(self, g):
        for h in range(2):
            self.copy(4, h, g, 0).wait_recv()
            self.rp2[h, g, 0] = plus(self.rp2[h, g, 0], self.part2[h, g, 4]).astype(BF)
            self.copy(6, h, g, 0).start()
            self.copy(5, h, g, 0).wait_recv()
            self.rm2[h, g, 1] = plus(self.rm2[h, g, 1], self.part2[h, g, 5]).astype(BF)
            self.copy(7, h, g, 0).start()

    def second_sum(self, h, g):
        self.copy(6, h, g, 0).wait_recv()
        self.copy(7, h, g, 0).wait_recv()
        return [
            plus(self.part2[h, g, 6], self.fp2[h, g], self.rm2[h, g, 0]),
            plus(self.part2[h, g, 7], self.fm2[h, g], self.rp2[h, g, 1]),
        ]

    def drain(self, g):
        for h in range(2):
            for k in range(RING):
                for which in range(4):
                    self.copy(which, h, g, k).wait_send()
            for which in range(4, 8):
                self.copy(which, h, g, 0).wait_send()


def kernel(act, cot, weight, first_in, second_in, anchor_in, mom_in, exps,
           w_out, f_out, s_out, anc_out, mom_out,
           a_v, c_v, w_v, f_v, s_v, anc_v, mom_v, wo_v, fo_v, so_v, ao_v, mo_v,
           wsum, rz, zt, zr, packs,
           a_sem, c_sem, in_sem, out_sem, z_s, z_r, zx_s, zx_r, k_s, k_r, *ring_refs):
    groups = c_v.shape[1] // GW
    last = groups - 1
    own = w_v.shape[0]
    block = 2 * own
    rep = lax.axis_index("rep")
    f = lax.axis_index("fsdp")
    zhi, x, y = f % 2, (f // 2) % RING, f // (2 * RING)

    def dev(x=x, y=y, zhi=zhi, rep=rep):
        return (rep, (y * RING + x) * 2 + zhi)

    xp, xm = dev(x=(x + 1) % RING), dev(x=(x + RING - 1) % RING)
    yp, ym = dev(y=(y + 1) % RING), dev(y=(y + RING - 1) % RING)
    zdev = dev(zhi=1 - zhi)
    mates = [dev(rep=(rep + i) % REPS) for i in range(1, REPS)]

    def cols(g):
        return pl.ds(pl.multiple_of(g * GW, GW), GW)

    def a_copy(blk):
        at = pl.ds(pl.multiple_of(blk * block, block), block)
        return pltpu.make_async_copy(act.at[0, :, at], a_v.at[:, at], a_sem.at[blk])

    def c_copy(g):
        return pltpu.make_async_copy(cot.at[0, :, cols(g)], c_v.at[:, cols(g)], c_sem.at[g])

    ins = [
        pltpu.make_async_copy(src, dst, in_sem.at[i])
        for i, (src, dst) in enumerate((
            (weight.at[0], w_v), (first_in.at[0], f_v), (second_in.at[0], s_v), (anchor_in, anc_v), (mom_in, mom_v)))
    ]

    def inner_outs(g):
        return [
            pltpu.make_async_copy(src.at[:, cols(g)], dst.at[0, :, cols(g)], out_sem.at[i, g])
            for i, (src, dst) in enumerate(((wo_v, w_out), (fo_v, f_out), (so_v, s_out)))
        ]

    def outer_outs(g):
        return [
            pltpu.make_async_copy(src.at[:, cols(g)], dst.at[:, cols(g)], out_sem.at[3 + i, g])
            for i, (src, dst) in enumerate(((ao_v, anc_out), (mo_v, mom_out)))
        ]

    def remote(src, dst, s, r, to):
        return pltpu.make_async_remote_copy(
            src_ref=src, dst_ref=dst, send_sem=s, recv_sem=r, device_id=to, device_id_type=MESH)

    def c_z(g):
        return remote(wsum.at[1 - zhi, g], rz.at[g], z_s.at[g], z_r.at[g], zdev)

    def c_zx(ry, rx):
        return remote(zt.at[ry, rx, 1 - zhi], zr.at[ry, rx], zx_s.at[ry, rx], zx_r.at[ry, rx], zdev)

    def c_pack(g, i):
        return remote(packs.at[g, rep], packs.at[g, rep], k_s.at[g, i], k_r.at[g, i], mates[i])

    wide = Rings(ring_refs[:26], (xp, yp), (xm, ym), remote)
    thin = Rings(ring_refs[26:], (xp, yp), (xm, ym), remote)

    def product(g, ry, rx):
        blk = ((y + OFFS[ry]) % RING) * RING + (x + OFFS[rx]) % RING
        at = pl.ds(pl.multiple_of(blk * block, block), block)
        return lax.dot_general(
            a_v[:, at], c_v[:, cols(g)], (((0,), (0,)), ((), ())), preferred_element_type=F32).astype(BF)

    def products(g, k):
        @pl.when(g == 0)
        def _():
            for ry, rx in NEW_BLOCKS[k]:
                a_copy(((y + OFFS[ry]) % RING) * RING + (x + OFFS[rx]) % RING).wait()

        if k == 0:
            c_copy(g).wait()
        for ry, rx in NEW_BLOCKS[k]:
            wide.place(g, ry, rx, product(g, ry, rx))
        wide.send(g, k)

        @pl.when(g == 0)
        def _():
            if k == 0:
                c_copy(last).wait()
            for ry, rx in NEW_BLOCKS[k]:
                tile = product(last, ry, rx)
                zt[ry, rx, 0] = tile[:own]
                zt[ry, rx, 1] = tile[own:]
                c_zx(ry, rx).start()

    def products_last(g, k):
        for ry, rx in NEW_BLOCKS[k]:
            c_zx(ry, rx).wait_recv()
            thin.place(0, ry, rx, plus(zt[ry, rx, zhi], zr[ry, rx]).astype(BF))
        thin.send(0, k)

    def second_sum(g):
        for h in range(2):
            wsum[h, g] = jnp.concatenate(wide.second_sum(h, g), axis=0).astype(BF)
        c_z(g).start()

    def powers(g):
        row = lax.broadcasted_iota(jnp.int32, (exps.shape[0], GW), 0)
        col = lax.broadcasted_iota(jnp.int32, (exps.shape[0], GW), 1)
        pick = jnp.where(row == g * (GW // 128) + col // 128, 1.0, 0.0).astype(BF)
        return lax.dot_general(
            exps[...].astype(F32).astype(BF), pick, (((0,), (0,)), ((), ())), preferred_element_type=F32)

    def adamw(g, grad):
        at = cols(g)
        first = (0.9 * f_v[:, at].astype(F32) + 0.1 * grad).astype(BF)
        second = (0.95 * s_v[:, at].astype(F32) + 0.05 * grad * grad).astype(BF)
        old = w_v[:, at].astype(F32)
        update = first.astype(F32) / (jnp.sqrt(second.astype(F32)) + 1e-08)
        fresh = (old - 0.1 * (update + 0.01 * old)).astype(BF)
        fo_v[:, at] = first
        so_v[:, at] = second
        wo_v[:, at] = fresh
        gap = anc_v[:, at].astype(F32) - fresh.astype(F32)
        packs[g, rep] = jnp.clip(gap * jnp.exp2(-powers(g)), -4.0, 4.0).astype(BF)
        for i in range(REPS - 1):
            c_pack(g, i).start()
        for copy in inner_outs(g):
            copy.start()

    def inner(g):
        c_z(g).wait_recv()
        @pl.when(g == 0)
        def _():
            for copy in ins:
                copy.wait()
        adamw(g, plus(wsum[zhi, g], rz[g]))

    def inner_last(g):
        adamw(last, jnp.concatenate(thin.second_sum(0, 0) + thin.second_sum(1, 0), axis=0))

    def outer(g):
        for i in range(REPS - 1):
            c_pack(g, i).wait_recv()
        at = cols(g)
        total = plus(*[packs[g, i] for i in range(REPS)])
        step = (jnp.exp2(powers(g)) * total) / REPS
        momentum = 0.9 * mom_v[:, at] + step
        mo_v[:, at] = momentum
        ao_v[:, at] = (anc_v[:, at].astype(F32) - 0.7 * (step + 0.9 * momentum)).astype(BF)
        for copy in outer_outs(g):
            copy.start()

    c_copy(0).start()
    for k in range(4):
        for ry, rx in NEW_BLOCKS[k]:
            a_copy(((y + OFFS[ry]) % RING) * RING + (x + OFFS[rx]) % RING).start()
        if k == 0:
            c_copy(last).start()
    for g in range(1, last):
        c_copy(g).start()
    for copy in ins:
        copy.start()

    everyone = [xp, xm, yp, ym, zdev] + mates
    barrier = pltpu.get_barrier_semaphore()
    for to in everyone:
        pl.semaphore_signal(barrier, inc=1, device_id=to, device_id_type=MESH)
    pl.semaphore_wait(barrier, len(everyone))

    def at_step(g, k, shift, stage, stage_last, only=None):
        group, kk = g + (k + shift) // 4, (k + shift) % 4
        if only is None or kk == only:
            rest = (kk,) if only is None else ()

            @pl.when(jnp.logical_and(group >= 0, group < last))
            def _():
                stage(group, *rest)

            if stage_last is not None:
                @pl.when(group == last)
                def _():
                    stage_last(0 if stage_last is not outer else group, *rest)

    first_turn = -((LEAD + 3) // 4)
    last_turn = -(-(LAGS[-1] + 3 + 1) // 4)

    @pl.loop(0, groups - first_turn + last_turn - 1)
    def _(turn):
        g = turn + first_turn
        for k in range(4):
            at_step(g, k, LEAD, products, products_last)
            at_step(g, k, FLEAD, wide.forward, thin.forward)
            at_step(g, k, 0, wide.first_sum, thin.first_sum)
            at_step(g, k, -LAGS[0], wide.forward2, thin.forward2, only=3)
            at_step(g, k, -LAGS[1], second_sum, None, only=3)
            at_step(g, k, -LAGS[2], inner, inner_last, only=3)
            at_step(g, k, -LAGS[3], outer, outer, only=3)

    @pl.loop(0, last)
    def _(g):
        wide.drain(g)
        c_z(g).wait_send()

    thin.drain(0)
    for ry in range(RING):
        for rx in range(RING):
            c_zx(ry, rx).wait_send()

    @pl.loop(0, groups)
    def _(g):
        for i in range(REPS - 1):
            c_pack(g, i).wait_send()
        for copy in inner_outs(g) + outer_outs(g):
            copy.wait()


def finish(*refs):
    sem = refs[-1]
    copies = [pltpu.make_async_copy(refs[i], refs[5 + i], sem.at[i]) for i in range(5)]
    for copy in copies:
        copy.start()
    for copy in copies:
        copy.wait()


def local(activations, cotangent, weight, first_moment, second_moment, anchor, momentum, exponents):
    own, width = anchor.shape
    tokens, rows = activations.shape[1:]
    groups = width // GW
    dma = pltpu.SemaphoreType.DMA
    anywhere = pl.BlockSpec(memory_space=pl.ANY)

    def buf(*shape, kind=BF):
        return pltpu.VMEM(shape, kind)

    def rings(count, unit):
        return [
            buf(2, count, RING, 8, unit, GW),
            buf(2, count, RING, 2, unit, GW), buf(2, count, RING, 2, unit, GW),
            buf(2, count, RING, unit, GW), buf(2, count, RING, unit, GW),
            buf(2, count, 8, unit, GW),
            buf(2, count, 2, unit, GW), buf(2, count, 2, unit, GW),
            buf(2, count, unit, GW), buf(2, count, unit, GW),
        ] + [dma((2, count, RING))] * 8 + [dma((2, count))] * 8

    outs = pl.pallas_call(
        kernel,
        out_shape=(
            jax.ShapeDtypeStruct(weight.shape, BF),
            jax.ShapeDtypeStruct(weight.shape, BF),
            jax.ShapeDtypeStruct(weight.shape, BF),
            jax.ShapeDtypeStruct(anchor.shape, BF),
            jax.ShapeDtypeStruct(momentum.shape, F32),
        ),
        in_specs=[anywhere] * 7 + [pl.BlockSpec(memory_space=pltpu.VMEM)],
        out_specs=[anywhere] * 5,
        scratch_shapes=[
            buf(tokens, rows), buf(tokens, width),
            buf(own, width), buf(own, width), buf(own, width), buf(own, width), buf(own, width, kind=F32),
            buf(own, width), buf(own, width), buf(own, width), buf(own, width), buf(own, width, kind=F32),
            buf(2, groups - 1, own, GW), buf(groups - 1, own, GW),
            buf(RING, RING, 2, own, GW), buf(RING, RING, own, GW), buf(groups, REPS, own, GW),
            dma((RING * RING,)), dma((groups,)), dma((5,)), dma((5, groups)),
            dma((groups - 1,)), dma((groups - 1,)), dma((RING, RING)), dma((RING, RING)),
            dma((groups, REPS - 1)), dma((groups, REPS - 1)),
        ] + rings(groups - 1, own // 2) + rings(1, own // 4),
        compiler_params=pltpu.CompilerParams(
            collective_id=0, has_side_effects=True, vmem_limit_bytes=58 * 1024 * 1024),
        cost_estimate=pl.CostEstimate(
            flops=2 * tokens * rows * width, bytes_accessed=12 * 2 ** 20, transcendentals=0),
        name="diloco_step",
    )(activations, cotangent, weight, first_moment, second_moment, anchor, momentum, exponents.T)
    return pl.pallas_call(
        finish,
        out_shape=[jax.ShapeDtypeStruct(o.shape, o.dtype) for o in outs],
        in_specs=[pl.BlockSpec(memory_space=pltpu.VMEM)] * 5,
        out_specs=[anywhere] * 5,
        scratch_shapes=[dma((5,))],
        name="results",
    )(*outs)


def solution(mesh):
    split = P("rep", "fsdp", None)
    rows = P("fsdp", None)
    return jax.shard_map(
        local,
        mesh=mesh,
        in_specs=(split, split, split, split, split, rows, rows, rows),
        out_specs=(split, split, split, rows, rows),
        check_vma=False,
    )
```

time: 111 us -> 91 us (0.82)
  local copies, waits for them, and re-layouts: 10.6 us -> 0 us
  Pallas kernels: 99.6 us -> 90.2 us
    pallas_call x1, Pallas kernels: 99.6 us -> 87.1 us  [local(): pl.pallas_call(kernel, out_shape=(jax.ShapeDtypeStruct(weight.shape, BF),...]
    unnamed x6 -> x0, local copies, waits for them, and re-layouts: 10.6 us -> none
    pallas_call x0 -> x1, Pallas kernels: none -> 3.05 us  [local(): pl.pallas_call(finish, out_shape=[jax.ShapeDtypeStruct(o.shape, o.dtype)...]
where the time goes in v2:
time: 91 us; the launch traced here: 90.8 us
  Pallas kernels  90.2 us (99%)
    pallas_call x1, Pallas kernels, local(): pl.pallas_call(kernel, out_shape=(jax.ShapeDtypeStruct(weight.shape, BF),...  87.1 us
    pallas_call x1, Pallas kernels, local(): pl.pallas_call(finish, out_shape=[jax.ShapeDtypeStruct(o.shape, o.dtype)...  3.05 us

profile of v2, /device:TPU:1, one launch (start us, length us, event | category | flops | bytes accessed | tf_op | source)
XLA Modules:
  0.0 90.8 jit_solution(9248765805599771453)
XLA Ops:
  0.6 87.1 %diloco_step.1 = (bf16[1,192,1024]{2,1,0:T(8,128)(2,1)}, bf16[1,192,1024]{2,1,0:T(8,128)(2,1)}, bf16[1,192,1024]{2,1,0:T(8,128)(2,1)}, bf16[192,1024]{1,0:T(8,128)(2,1)}, f32[192,1024]{1,0:T(8,128)}) custom-call(bf16[1,512,6144]{2,1,0:T(8,128)(2,1)} %act.1, bf16[1,512,1024]{2,1,0:T(8,128)(2,1)} %cot.1, bf16[1,192,1024]{2,1,0:T(8,128)(2,1)} %weight.1, ...), custom_call_target="tpu_custom_call" | custom-call | flops 6442450944 | bytes 12582912 | tf_op jit(solution)/shard_map/diloco_step/pallas_call | solution.py:362
  87.8 3.1 %results.1 = (bf16[1,192,1024]{2,1,0:T(8,128)(2,1)}, bf16[1,192,1024]{2,1,0:T(8,128)(2,1)}, bf16[1,192,1024]{2,1,0:T(8,128)(2,1)}, bf16[192,1024]{1,0:T(8,128)(2,1)}, f32[192,1024]{1,0:T(8,128)}) custom-call(bf16[1,192,1024]{2,1,0:T(8,128)(2,1)} %get-tuple-element.10.refs_0_, bf16[1,192,1024]{2,1,0:T(8,128)(2,1)} %get-tuple-element.11.refs_1_, ...), custom_call_target="tpu_custom_call" | custom-call | tf_op jit(solution)/shard_map/results/pallas_call | solution.py:389

commit v3 on v2

--- a/solution.py
+++ b/solution.py
@@ -12,9 +12,11 @@
 RING = 4
 REPS = 4
 GW = 256
-LEAD = 4
-FLEAD = 2
-LAGS = (1,3,5,7)
+LEADS = (4, 4)
+FLEADS = (2, 2)
+LAGS = (1, 3, 5, 6, 7)
+LAST_LAGS = (1, 2, 3, 4)
+EXCHANGE = -3
 OFFS = (2, 1, 3, 0)
 A_SLOT = (0, 4, 2, 6)
 B_SLOT = (3, 1, 5, 7)
@@ -24,6 +26,9 @@
     ((2, 2), (0, 3), (3, 0)),
     ((3, 1), (3, 2), (1, 3), (2, 3), (3, 3)),
 )
+SEND_AFTER = ((3, 5), (2, 3), (1, 1), (2, 4))
+FLAT = sum(NEW_BLOCKS, ())
+BATCHES = tuple(FLAT[i:i + 2] for i in range(0, 16, 2))
 
 
 def plus(*terms):
@@ -63,10 +68,9 @@
         self.part[1, g, rx, A_SLOT[ry]] = tile[2 * u:3 * u]
         self.part[1, g, rx, B_SLOT[ry]] = tile[3 * u:]
 
-    def send(self, g, k):
-        for h in range(2):
-            self.copy(0, h, g, k).start()
-            self.copy(1, h, g, k).start()
+    def send(self, h, g, k):
+        self.copy(0, h, g, k).start()
+        self.copy(1, h, g, k).start()
 
     def forward(self, g, k):
         for h in range(2):
@@ -118,7 +122,7 @@
 def kernel(act, cot, weight, first_in, second_in, anchor_in, mom_in, exps,
            w_out, f_out, s_out, anc_out, mom_out,
            a_v, c_v, w_v, f_v, s_v, anc_v, mom_v, wo_v, fo_v, so_v, ao_v, mo_v,
-           wsum, rz, zt, zr, packs,
+           wsum, rz, zt, zr, packs, pairs,
            a_sem, c_sem, in_sem, out_sem, z_s, z_r, zx_s, zx_r, k_s, k_r, *ring_refs):
     groups = c_v.shape[1] // GW
     last = groups - 1
@@ -134,7 +138,9 @@
     xp, xm = dev(x=(x + 1) % RING), dev(x=(x + RING - 1) % RING)
     yp, ym = dev(y=(y + 1) % RING), dev(y=(y + RING - 1) % RING)
     zdev = dev(zhi=1 - zhi)
-    mates = [dev(rep=(rep + i) % REPS) for i in range(1, REPS)]
+    zlo, core = rep // 2, rep % 2
+    mate = dev(rep=2 * zlo + 1 - core)
+    across = dev(rep=2 * (1 - zlo) + core), dev(rep=2 * (1 - zlo) + 1 - core)
 
     def cols(g):
         return pl.ds(pl.multiple_of(g * GW, GW), GW)
@@ -174,8 +180,12 @@
     def c_zx(ry, rx):
         return remote(zt.at[ry, rx, 1 - zhi], zr.at[ry, rx], zx_s.at[ry, rx], zx_r.at[ry, rx], zdev)
 
-    def c_pack(g, i):
-        return remote(packs.at[g, rep], packs.at[g, rep], k_s.at[g, i], k_r.at[g, i], mates[i])
+    def c_pack(g):
+        return remote(packs.at[g, core], packs.at[g, core], k_s.at[g, 0], k_r.at[g, 0], mate)
+
+    def c_pair(g, i):
+        here = pairs.at[g, zlo, core]
+        return remote(here, here, k_s.at[g, 1 + i], k_r.at[g, 1 + i], across[i])
 
     wide = Rings(ring_refs[:26], (xp, yp), (xm, ym), remote)
     thin = Rings(ring_refs[26:], (xp, yp), (xm, ym), remote)
@@ -194,25 +204,36 @@
 
         if k == 0:
             c_copy(g).wait()
-        for ry, rx in NEW_BLOCKS[k]:
+        for n, (ry, rx) in enumerate(NEW_BLOCKS[k]):
             wide.place(g, ry, rx, product(g, ry, rx))
-        wide.send(g, k)
-
-        @pl.when(g == 0)
-        def _():
-            if k == 0:
-                c_copy(last).wait()
-            for ry, rx in NEW_BLOCKS[k]:
-                tile = product(last, ry, rx)
-                zt[ry, rx, 0] = tile[:own]
-                zt[ry, rx, 1] = tile[own:]
-                c_zx(ry, rx).start()
+            for h in range(2):
+                if n + 1 == SEND_AFTER[k][h]:
+                    if k == 0 and h == 0:
+                        @pl.when(g == 0)
+                        def _():
+                            pl.semaphore_wait(barrier, len(everyone))
+                    wide.send(h, g, k)
+        if k == 0:
+            @pl.when(g == 0)
+            def _():
+                load_rest()
+
+    def exchange(n):
+        if n == 0:
+            c_copy(last).wait()
+        for ry, rx in BATCHES[n]:
+            tile = product(last, ry, rx)
+            zt[ry, rx, 0] = tile[:own]
+            zt[ry, rx, 1] = tile[own:]
+            c_zx(ry, rx).start()
 
     def products_last(g, k):
-        for ry, rx in NEW_BLOCKS[k]:
+        for n, (ry, rx) in enumerate(NEW_BLOCKS[k]):
             c_zx(ry, rx).wait_recv()
             thin.place(0, ry, rx, plus(zt[ry, rx, zhi], zr[ry, rx]).astype(BF))
-        thin.send(0, k)
+            for h in range(2):
+                if n + 1 == SEND_AFTER[k][h]:
+                    thin.send(h, 0, k)
 
     def second_sum(g):
         for h in range(2):
@@ -237,9 +258,8 @@
         so_v[:, at] = second
         wo_v[:, at] = fresh
         gap = anc_v[:, at].astype(F32) - fresh.astype(F32)
-        packs[g, rep] = jnp.clip(gap * jnp.exp2(-powers(g)), -4.0, 4.0).astype(BF)
-        for i in range(REPS - 1):
-            c_pack(g, i).start()
+        packs[g, core] = jnp.clip(gap * jnp.exp2(-powers(g)), -4.0, 4.0).astype(BF)
+        c_pack(g).start()
         for copy in inner_outs(g):
             copy.start()
 
@@ -251,14 +271,31 @@
                 copy.wait()
         adamw(g, plus(wsum[zhi, g], rz[g]))
 
+    def thin_forward(g, k):
+        thin.forward(0, k)
+
+    def thin_first_sum(g, k):
+        thin.first_sum(0, k)
+
+    def thin_forward2(g):
+        thin.forward2(0)
+
     def inner_last(g):
         adamw(last, jnp.concatenate(thin.second_sum(0, 0) + thin.second_sum(1, 0), axis=0))
 
+    def pair(g):
+        c_pack(g).wait_recv()
+        both = plus(packs[g, 0], packs[g, 1]).astype(BF)
+        pairs[g, zlo, 0] = both[:own // 2]
+        pairs[g, zlo, 1] = both[own // 2:]
+        for i in range(2):
+            c_pair(g, i).start()
+
     def outer(g):
-        for i in range(REPS - 1):
-            c_pack(g, i).wait_recv()
+        for i in range(2):
+            c_pair(g, i).wait_recv()
         at = cols(g)
-        total = plus(*[packs[g, i] for i in range(REPS)])
+        total = jnp.concatenate([plus(pairs[g, 0, i], pairs[g, 1, i]) for i in range(2)], axis=0)
         step = (jnp.exp2(powers(g)) * total) / REPS
         momentum = 0.9 * mom_v[:, at] + step
         mo_v[:, at] = momentum
@@ -266,51 +303,64 @@
         for copy in outer_outs(g):
             copy.start()
 
-    c_copy(0).start()
-    for k in range(4):
-        for ry, rx in NEW_BLOCKS[k]:
-            a_copy(((y + OFFS[ry]) % RING) * RING + (x + OFFS[rx]) % RING).start()
-        if k == 0:
-            c_copy(last).start()
-    for g in range(1, last):
-        c_copy(g).start()
-    for copy in ins:
-        copy.start()
-
-    everyone = [xp, xm, yp, ym, zdev] + mates
+    everyone = [xp, xm, yp, ym, zdev, mate, *across]
     barrier = pltpu.get_barrier_semaphore()
     for to in everyone:
         pl.semaphore_signal(barrier, inc=1, device_id=to, device_id_type=MESH)
-    pl.semaphore_wait(barrier, len(everyone))
-
-    def at_step(g, k, shift, stage, stage_last, only=None):
-        group, kk = g + (k + shift) // 4, (k + shift) % 4
-        if only is None or kk == only:
-            rest = (kk,) if only is None else ()
-
-            @pl.when(jnp.logical_and(group >= 0, group < last))
+
+    def load(k):
+        for ry, rx in NEW_BLOCKS[k]:
+            a_copy(((y + OFFS[ry]) % RING) * RING + (x + OFFS[rx]) % RING).start()
+
+    def load_rest():
+        for k in range(1, RING):
+            load(k)
+        for g in (last, *range(1, last)):
+            c_copy(g).start()
+        for copy in ins:
+            copy.start()
+
+    c_copy(0).start()
+    load(0)
+
+    def at_step(g, k, shift, stage, groups_of, *late):
+        group, kk = g + (k + shift) // RING, (k + shift) % RING
+        if not late or kk == RING - 1:
+            @pl.when(groups_of(group))
             def _():
-                stage(group, *rest)
-
-            if stage_last is not None:
-                @pl.when(group == last)
-                def _():
-                    stage_last(0 if stage_last is not outer else group, *rest)
-
-    first_turn = -((LEAD + 3) // 4)
-    last_turn = -(-(LAGS[-1] + 3 + 1) // 4)
+                stage(group) if late else stage(group, kk)
+
+    def is_wide(group):
+        return jnp.logical_and(group >= 0, group < last)
+
+    def is_last(group):
+        return group == last
+
+    first_turn = -((max(LEADS) + RING - 1) // RING)
+    end = max(LAGS[-1] - RING, LAST_LAGS[-1])
+    last_turn = -(-(end + RING) // RING)
 
     @pl.loop(0, groups - first_turn + last_turn - 1)
     def _(turn):
         g = turn + first_turn
-        for k in range(4):
-            at_step(g, k, LEAD, products, products_last)
-            at_step(g, k, FLEAD, wide.forward, thin.forward)
-            at_step(g, k, 0, wide.first_sum, thin.first_sum)
-            at_step(g, k, -LAGS[0], wide.forward2, thin.forward2, only=3)
-            at_step(g, k, -LAGS[1], second_sum, None, only=3)
-            at_step(g, k, -LAGS[2], inner, inner_last, only=3)
-            at_step(g, k, -LAGS[3], outer, outer, only=3)
+        for k in range(RING):
+            at_step(g, k, LEADS[0], products, is_wide)
+            at_step(g, k, LEADS[1], products_last, is_last)
+            for n in range(len(BATCHES)):
+                step = n + EXCHANGE
+                if step % RING == k:
+                    @pl.when(g == step // RING)
+                    def _():
+                        exchange(n)
+
+            at_step(g, k, FLEADS[0], wide.forward, is_wide)
+            at_step(g, k, FLEADS[1], thin_forward, is_last)
+            at_step(g, k, 0, wide.first_sum, is_wide)
+            at_step(g, k, 0, thin_first_sum, is_last)
+            for lag, stage in zip(LAST_LAGS, (thin_forward2, inner_last, pair, outer)):
+                at_step(g, k, -lag, stage, is_last, "late")
+            for lag, stage in zip(LAGS, (wide.forward2, second_sum, inner, pair, outer)):
+                at_step(g, k, -lag, stage, is_wide, "late")
 
     @pl.loop(0, last)
     def _(g):
@@ -324,18 +374,24 @@
 
     @pl.loop(0, groups)
     def _(g):
-        for i in range(REPS - 1):
-            c_pack(g, i).wait_send()
+        c_pack(g).wait_send()
+        for i in range(2):
+            c_pair(g, i).wait_send()
         for copy in inner_outs(g) + outer_outs(g):
             copy.wait()
 
 
 def finish(*refs):
-    sem = refs[-1]
-    copies = [pltpu.make_async_copy(refs[i], refs[5 + i], sem.at[i]) for i in range(5)]
-    for copy in copies:
+    given, made, held = refs[:5], refs[5:10], refs[10:15]
+    sem = refs[15]
+    inward = [pltpu.make_async_copy(given[i], held[i], sem.at[0, i]) for i in range(5)]
+    outward = [pltpu.make_async_copy(held[i], made[i], sem.at[1, i]) for i in range(5)]
+    for copy in inward:
         copy.start()
-    for copy in copies:
+    for arrived, copy in zip(inward, outward):
+        arrived.wait()
+        copy.start()
+    for copy in outward:
         copy.wait()
 
 
@@ -375,10 +431,11 @@
             buf(own, width), buf(own, width), buf(own, width), buf(own, width), buf(own, width, kind=F32),
             buf(own, width), buf(own, width), buf(own, width), buf(own, width), buf(own, width, kind=F32),
             buf(2, groups - 1, own, GW), buf(groups - 1, own, GW),
-            buf(RING, RING, 2, own, GW), buf(RING, RING, own, GW), buf(groups, REPS, own, GW),
+            buf(RING, RING, 2, own, GW), buf(RING, RING, own, GW),
+            buf(groups, 2, own, GW), buf(groups, 2, 2, own // 2, GW),
             dma((RING * RING,)), dma((groups,)), dma((5,)), dma((5, groups)),
             dma((groups - 1,)), dma((groups - 1,)), dma((RING, RING)), dma((RING, RING)),
-            dma((groups, REPS - 1)), dma((groups, REPS - 1)),
+            dma((groups, 3)), dma((groups, 3)),
         ] + rings(groups - 1, own // 2) + rings(1, own // 4),
         compiler_params=pltpu.CompilerParams(
             collective_id=0, has_side_effects=True, vmem_limit_bytes=58 * 1024 * 1024),
@@ -389,9 +446,9 @@
     return pl.pallas_call(
         finish,
         out_shape=[jax.ShapeDtypeStruct(o.shape, o.dtype) for o in outs],
-        in_specs=[pl.BlockSpec(memory_space=pltpu.VMEM)] * 5,
+        in_specs=[anywhere] * 5,
         out_specs=[anywhere] * 5,
-        scratch_shapes=[dma((5,))],
+        scratch_shapes=[buf(*o.shape, kind=o.dtype) for o in outs] + [dma((2, 5))],
         name="results",
     )(*outs)
 

time: 91 us -> 86.1 us (0.946)
  Pallas kernels: 90.2 us -> 85.3 us
    pallas_call x1, Pallas kernels: 87.1 us -> 82.7 us  [local(): pl.pallas_call(kernel, out_shape=(jax.ShapeDtypeStruct(weight.shape, BF),...]
where the time goes in v3:
time: 86.1 us; the launch traced here: 85.9 us
  Pallas kernels  85.3 us (99%)
    pallas_call x1, Pallas kernels, local(): pl.pallas_call(kernel, out_shape=(jax.ShapeDtypeStruct(weight.shape, BF),...  82.7 us
    pallas_call x1, Pallas kernels, local(): pl.pallas_call(finish, out_shape=[jax.ShapeDtypeStruct(o.shape, o.dtype)...  2.58 us

profile of v3, /device:TPU:1, one launch (start us, length us, event | category | flops | bytes accessed | tf_op | source)
XLA Modules:
  0.0 85.9 jit_solution(10376608772085272714)
XLA Ops:
  0.6 82.7 %diloco_step.1 = (bf16[1,192,1024]{2,1,0:T(8,128)(2,1)}, bf16[1,192,1024]{2,1,0:T(8,128)(2,1)}, bf16[1,192,1024]{2,1,0:T(8,128)(2,1)}, bf16[192,1024]{1,0:T(8,128)(2,1)}, f32[192,1024]{1,0:T(8,128)}) custom-call(bf16[1,512,6144]{2,1,0:T(8,128)(2,1)} %act.1, bf16[1,512,1024]{2,1,0:T(8,128)(2,1)} %cot.1, bf16[1,192,1024]{2,1,0:T(8,128)(2,1)} %weight.1, ...), custom_call_target="tpu_custom_call" | custom-call | flops 6442450944 | bytes 12582912 | tf_op jit(solution)/shard_map/diloco_step/pallas_call | solution.py:418
  83.3 2.6 %results.1 = (bf16[1,192,1024]{2,1,0:T(8,128)(2,1)}, bf16[1,192,1024]{2,1,0:T(8,128)(2,1)}, bf16[1,192,1024]{2,1,0:T(8,128)(2,1)}, bf16[192,1024]{1,0:T(8,128)(2,1)}, f32[192,1024]{1,0:T(8,128)}) custom-call(bf16[1,192,1024]{2,1,0:T(8,128)(2,1)} %get-tuple-element.10.refs_0_, bf16[1,192,1024]{2,1,0:T(8,128)(2,1)} %get-tuple-element.11.refs_1_, ...), custom_call_target="tpu_custom_call" | custom-call | tf_op jit(solution)/shard_map/results/pallas_call | solution.py:446

commit v4 on v3

--- a/solution.py
+++ b/solution.py
@@ -14,8 +14,8 @@
 GW = 256
 LEADS = (4, 4)
 FLEADS = (2, 2)
-LAGS = (1, 3, 5, 6, 7)
-LAST_LAGS = (1, 2, 3, 4)
+LAGS = (1, 3, 5, 6, 7, 7)
+END = ((0, "forward"), (1, "sum"), (3, "inner_last"), (3, "inner"), (4, "pair_last"), (4, "pair"), (4, "tidy_last"), (4, "tidy"), (4, "outer_last"), (4, "outer"))
 EXCHANGE = -3
 OFFS = (2, 1, 3, 0)
 A_SLOT = (0, 4, 2, 6)
@@ -119,10 +119,44 @@
                 self.copy(which, h, g, 0).wait_send()
 
 
-def kernel(act, cot, weight, first_in, second_in, anchor_in, mom_in, exps,
+class ShortRings(Rings):
+    def __init__(self, refs, up, down, owners, remote):
+        self.part, self.rp, self.rm, self.fp, self.fm, self.part2, self.got = refs[:7]
+        self.sems, self.q_s, self.q_r = refs[7:15], refs[15], refs[16]
+        self.up, self.down, self.owners, self.remote = up, down, owners, remote
+        self.unit = self.part.shape[-2]
+
+    def straight(self, h, k):
+        return self.remote(
+            self.part2.at[h, k], self.got.at[h, k], self.q_s.at[h, k], self.q_r.at[h, k], self.owners[1 - h][k])
+
+    def first_sum(self, g, k):
+        for h in range(2):
+            self.copy(2, h, g, k).wait_recv()
+            self.copy(3, h, g, k).wait_recv()
+            self.part2[h, k, 0] = plus(self.part[h, g, k, 6], self.fp[h, g, k], self.rm[h, g, k, 0]).astype(BF)
+            self.part2[h, k, 1] = plus(self.part[h, g, k, 7], self.fm[h, g, k], self.rp[h, g, k, 1]).astype(BF)
+            if k < 3:
+                self.straight(h, k).start()
+
+    def second_sum(self, h, g):
+        for k in range(3):
+            self.straight(h, k).wait_recv()
+        return [plus(self.part2[h, 3, i], *[self.got[h, k, i] for k in range(3)]) for i in range(2)]
+
+    def drain(self, g):
+        for h in range(2):
+            for k in range(RING):
+                for which in range(4):
+                    self.copy(which, h, g, k).wait_send()
+            for k in range(3):
+                self.straight(h, k).wait_send()
+
+
+def kernel(act, cot, weight, first_in, second_in, anchor_in, mom_in, exps_in,
            w_out, f_out, s_out, anc_out, mom_out,
            a_v, c_v, w_v, f_v, s_v, anc_v, mom_v, wo_v, fo_v, so_v, ao_v, mo_v,
-           wsum, rz, zt, zr, packs, pairs,
+           exps, wsum, rz, zt, zr, packs, pairs,
            a_sem, c_sem, in_sem, out_sem, z_s, z_r, zx_s, zx_r, k_s, k_r, *ring_refs):
     groups = c_v.shape[1] // GW
     last = groups - 1
@@ -137,6 +171,7 @@
 
     xp, xm = dev(x=(x + 1) % RING), dev(x=(x + RING - 1) % RING)
     yp, ym = dev(y=(y + 1) % RING), dev(y=(y + RING - 1) % RING)
+    x2, y2 = dev(x=(x + 2) % RING), dev(y=(y + 2) % RING)
     zdev = dev(zhi=1 - zhi)
     zlo, core = rep // 2, rep % 2
     mate = dev(rep=2 * zlo + 1 - core)
@@ -155,7 +190,8 @@
     ins = [
         pltpu.make_async_copy(src, dst, in_sem.at[i])
         for i, (src, dst) in enumerate((
-            (weight.at[0], w_v), (first_in.at[0], f_v), (second_in.at[0], s_v), (anchor_in, anc_v), (mom_in, mom_v)))
+            (weight.at[0], w_v), (first_in.at[0], f_v), (second_in.at[0], s_v), (anchor_in, anc_v), (mom_in, mom_v),
+            (exps_in, exps)))
     ]
 
     def inner_outs(g):
@@ -188,7 +224,7 @@
         return remote(here, here, k_s.at[g, 1 + i], k_r.at[g, 1 + i], across[i])
 
     wide = Rings(ring_refs[:26], (xp, yp), (xm, ym), remote)
-    thin = Rings(ring_refs[26:], (xp, yp), (xm, ym), remote)
+    thin = ShortRings(ring_refs[26:], (xp, yp), (xm, ym), ((x2, xp, xm), (y2, yp, ym)), remote)
 
     def product(g, ry, rx):
         blk = ((y + OFFS[ry]) % RING) * RING + (x + OFFS[rx]) % RING
@@ -277,9 +313,6 @@
     def thin_first_sum(g, k):
         thin.first_sum(0, k)
 
-    def thin_forward2(g):
-        thin.forward2(0)
-
     def inner_last(g):
         adamw(last, jnp.concatenate(thin.second_sum(0, 0) + thin.second_sum(1, 0), axis=0))
 
@@ -303,7 +336,30 @@
         for copy in outer_outs(g):
             copy.start()
 
-    everyone = [xp, xm, yp, ym, zdev, mate, *across]
+    def tidy(g):
+        wide.drain(g)
+        c_z(g).wait_send()
+        c_pack(g).wait_send()
+        for i in range(2):
+            c_pair(g, i).wait_send()
+
+    def tidy_last(g):
+        thin.drain(0)
+        for ry in range(RING):
+            for rx in range(RING):
+                c_zx(ry, rx).wait_send()
+        c_pack(g).wait_send()
+        for i in range(2):
+            c_pair(g, i).wait_send()
+
+    before = last - 1
+    ends = dict(
+        forward=lambda: wide.forward2(before), sum=lambda: second_sum(before), inner=lambda: inner(before),
+        pair=lambda: pair(before), outer=lambda: outer(before), tidy=lambda: tidy(before),
+        inner_last=lambda: inner_last(last), pair_last=lambda: pair(last), outer_last=lambda: outer(last),
+        tidy_last=lambda: tidy_last(last))
+
+    everyone = [xp, xm, x2, yp, ym, y2, zdev, mate, *across]
     barrier = pltpu.get_barrier_semaphore()
     for to in everyone:
         pl.semaphore_signal(barrier, inc=1, device_id=to, device_id_type=MESH)
@@ -333,14 +389,16 @@
     def is_wide(group):
         return jnp.logical_and(group >= 0, group < last)
 
+    def is_early(group):
+        return jnp.logical_and(group >= 0, group < last - 1)
+
     def is_last(group):
         return group == last
 
     first_turn = -((max(LEADS) + RING - 1) // RING)
-    end = max(LAGS[-1] - RING, LAST_LAGS[-1])
-    last_turn = -(-(end + RING) // RING)
-
-    @pl.loop(0, groups - first_turn + last_turn - 1)
+    last_turn = END[-1][0] // RING
+
+    @pl.loop(0, groups - first_turn + last_turn)
     def _(turn):
         g = turn + first_turn
         for k in range(RING):
@@ -357,26 +415,16 @@
             at_step(g, k, FLEADS[1], thin_forward, is_last)
             at_step(g, k, 0, wide.first_sum, is_wide)
             at_step(g, k, 0, thin_first_sum, is_last)
-            for lag, stage in zip(LAST_LAGS, (thin_forward2, inner_last, pair, outer)):
-                at_step(g, k, -lag, stage, is_last, "late")
-            for lag, stage in zip(LAGS, (wide.forward2, second_sum, inner, pair, outer)):
-                at_step(g, k, -lag, stage, is_wide, "late")
-
-    @pl.loop(0, last)
-    def _(g):
-        wide.drain(g)
-        c_z(g).wait_send()
-
-    thin.drain(0)
-    for ry in range(RING):
-        for rx in range(RING):
-            c_zx(ry, rx).wait_send()
-
-    @pl.loop(0, groups)
-    def _(g):
-        c_pack(g).wait_send()
-        for i in range(2):
-            c_pair(g, i).wait_send()
+            for lag, stage in zip(LAGS, (wide.forward2, second_sum, inner, pair, outer, tidy)):
+                at_step(g, k, -lag, stage, is_early, "late")
+            for step, stage in END:
+                if step % RING == k:
+                    @pl.when(g == last + step // RING)
+                    def _():
+                        ends[stage]()
+
+
+    for g in range(groups):
         for copy in inner_outs(g) + outer_outs(g):
             copy.wait()
 
@@ -415,6 +463,14 @@
             buf(2, count, unit, GW), buf(2, count, unit, GW),
         ] + [dma((2, count, RING))] * 8 + [dma((2, count))] * 8
 
+    def short_rings(unit):
+        return [
+            buf(2, 1, RING, 8, unit, GW),
+            buf(2, 1, RING, 2, unit, GW), buf(2, 1, RING, 2, unit, GW),
+            buf(2, 1, RING, unit, GW), buf(2, 1, RING, unit, GW),
+            buf(2, RING, 2, unit, GW), buf(2, RING - 1, 2, unit, GW),
+        ] + [dma((2, 1, RING))] * 8 + [dma((2, RING - 1))] * 2
+
     outs = pl.pallas_call(
         kernel,
         out_shape=(
@@ -424,19 +480,20 @@
             jax.ShapeDtypeStruct(anchor.shape, BF),
             jax.ShapeDtypeStruct(momentum.shape, F32),
         ),
-        in_specs=[anywhere] * 7 + [pl.BlockSpec(memory_space=pltpu.VMEM)],
+        in_specs=[anywhere] * 8,
         out_specs=[anywhere] * 5,
         scratch_shapes=[
             buf(tokens, rows), buf(tokens, width),
             buf(own, width), buf(own, width), buf(own, width), buf(own, width), buf(own, width, kind=F32),
             buf(own, width), buf(own, width), buf(own, width), buf(own, width), buf(own, width, kind=F32),
+            buf(*exponents.shape[::-1], kind=jnp.int32),
             buf(2, groups - 1, own, GW), buf(groups - 1, own, GW),
             buf(RING, RING, 2, own, GW), buf(RING, RING, own, GW),
             buf(groups, 2, own, GW), buf(groups, 2, 2, own // 2, GW),
-            dma((RING * RING,)), dma((groups,)), dma((5,)), dma((5, groups)),
+            dma((RING * RING,)), dma((groups,)), dma((6,)), dma((5, groups)),
             dma((groups - 1,)), dma((groups - 1,)), dma((RING, RING)), dma((RING, RING)),
             dma((groups, 3)), dma((groups, 3)),
-        ] + rings(groups - 1, own // 2) + rings(1, own // 4),
+        ] + rings(groups - 1, own // 2) + short_rings(own // 4),
         compiler_params=pltpu.CompilerParams(
             collective_id=0, has_side_effects=True, vmem_limit_bytes=58 * 1024 * 1024),
         cost_estimate=pl.CostEstimate(

time: 86.1 us -> 83.9 us (0.974)
  Pallas kernels: 85.3 us -> 83.1 us
    pallas_call x1, Pallas kernels: 82.7 us -> 80.5 us  [local(): pl.pallas_call(kernel, out_shape=(jax.ShapeDtypeStruct(weight.shape, BF),...]
where the time goes in v4:
time: 83.9 us; the launch traced here: 83.7 us
  Pallas kernels  83.1 us (99%)
    pallas_call x1, Pallas kernels, local(): pl.pallas_call(kernel, out_shape=(jax.ShapeDtypeStruct(weight.shape, BF),...  80.5 us
    pallas_call x1, Pallas kernels, local(): pl.pallas_call(finish, out_shape=[jax.ShapeDtypeStruct(o.shape, o.dtype)...  2.58 us

profile of v4, /device:TPU:1, one launch (start us, length us, event | category | flops | bytes accessed | tf_op | source)
XLA Modules:
  0.0 83.7 jit_solution(3395126479673166647)
XLA Ops:
  0.6 80.5 %diloco_step.1 = (bf16[1,192,1024]{2,1,0:T(8,128)(2,1)}, bf16[1,192,1024]{2,1,0:T(8,128)(2,1)}, bf16[1,192,1024]{2,1,0:T(8,128)(2,1)}, bf16[192,1024]{1,0:T(8,128)(2,1)}, f32[192,1024]{1,0:T(8,128)}) custom-call(bf16[1,512,6144]{2,1,0:T(8,128)(2,1)} %act.1, bf16[1,512,1024]{2,1,0:T(8,128)(2,1)} %cot.1, bf16[1,192,1024]{2,1,0:T(8,128)(2,1)} %weight.1, ...), custom_call_target="tpu_custom_call" | custom-call | flops 6442450944 | bytes 12582912 | tf_op jit(solution)/shard_map/diloco_step/pallas_call | solution.py:474
  81.1 2.6 %results.1 = (bf16[1,192,1024]{2,1,0:T(8,128)(2,1)}, bf16[1,192,1024]{2,1,0:T(8,128)(2,1)}, bf16[1,192,1024]{2,1,0:T(8,128)(2,1)}, bf16[192,1024]{1,0:T(8,128)(2,1)}, f32[192,1024]{1,0:T(8,128)}) custom-call(bf16[1,192,1024]{2,1,0:T(8,128)(2,1)} %get-tuple-element.10.refs_0_, bf16[1,192,1024]{2,1,0:T(8,128)(2,1)} %get-tuple-element.11.refs_1_, ...), custom_call_target="tpu_custom_call" | custom-call | tf_op jit(solution)/shard_map/results/pallas_call | solution.py:503

commit v5 on v4

--- a/solution.py
+++ b/solution.py
@@ -14,8 +14,8 @@
 GW = 256
 LEADS = (4, 4)
 FLEADS = (2, 2)
-LAGS = (1, 3, 5, 6, 7, 7)
-END = ((0, "forward"), (1, "sum"), (3, "inner_last"), (3, "inner"), (4, "pair_last"), (4, "pair"), (4, "tidy_last"), (4, "tidy"), (4, "outer_last"), (4, "outer"))
+LAGS = (1, 3, 5, 6, 7, 7, 7)
+END = ((0, "forward"), (1, "sum"), (3, "inner_last"), (3, "inner"), (4, "pair_last"), (4, "pair"), (4, "tidy_last"), (4, "tidy"), (4, "share_last"), (4, "share"), (4, "outer_last"), (4, "outer"))
 EXCHANGE = -3
 OFFS = (2, 1, 3, 0)
 A_SLOT = (0, 4, 2, 6)
@@ -156,7 +156,7 @@
 def kernel(act, cot, weight, first_in, second_in, anchor_in, mom_in, exps_in,
            w_out, f_out, s_out, anc_out, mom_out,
            a_v, c_v, w_v, f_v, s_v, anc_v, mom_v, wo_v, fo_v, so_v, ao_v, mo_v,
-           exps, wsum, rz, zt, zr, packs, pairs,
+           exps, wsum, rz, zt, zr, packs, pairs, totals,
            a_sem, c_sem, in_sem, out_sem, z_s, z_r, zx_s, zx_r, k_s, k_r, *ring_refs):
     groups = c_v.shape[1] // GW
     last = groups - 1
@@ -175,7 +175,7 @@
     zdev = dev(zhi=1 - zhi)
     zlo, core = rep // 2, rep % 2
     mate = dev(rep=2 * zlo + 1 - core)
-    across = dev(rep=2 * (1 - zlo) + core), dev(rep=2 * (1 - zlo) + 1 - core)
+    across = dev(rep=2 * (1 - zlo) + core)
 
     def cols(g):
         return pl.ds(pl.multiple_of(g * GW, GW), GW)
@@ -217,11 +217,16 @@
         return remote(zt.at[ry, rx, 1 - zhi], zr.at[ry, rx], zx_s.at[ry, rx], zx_r.at[ry, rx], zdev)
 
     def c_pack(g):
-        return remote(packs.at[g, core], packs.at[g, core], k_s.at[g, 0], k_r.at[g, 0], mate)
-
-    def c_pair(g, i):
-        here = pairs.at[g, zlo, core]
-        return remote(here, here, k_s.at[g, 1 + i], k_r.at[g, 1 + i], across[i])
+        here = packs.at[g, core, 1 - core]
+        return remote(here, here, k_s.at[g, 0], k_r.at[g, 0], mate)
+
+    def c_pair(g):
+        here = pairs.at[g, zlo]
+        return remote(here, here, k_s.at[g, 1], k_r.at[g, 1], across)
+
+    def c_share(g):
+        here = totals.at[g, core]
+        return remote(here, here, k_s.at[g, 2], k_r.at[g, 2], mate)
 
     wide = Rings(ring_refs[:26], (xp, yp), (xm, ym), remote)
     thin = ShortRings(ring_refs[26:], (xp, yp), (xm, ym), ((x2, xp, xm), (y2, yp, ym)), remote)
@@ -294,7 +299,9 @@
         so_v[:, at] = second
         wo_v[:, at] = fresh
         gap = anc_v[:, at].astype(F32) - fresh.astype(F32)
-        packs[g, core] = jnp.clip(gap * jnp.exp2(-powers(g)), -4.0, 4.0).astype(BF)
+        pack = jnp.clip(gap * jnp.exp2(-powers(g)), -4.0, 4.0).astype(BF)
+        packs[g, core, 0] = pack[:own // 2]
+        packs[g, core, 1] = pack[own // 2:]
         c_pack(g).start()
         for copy in inner_outs(g):
             copy.start()
@@ -318,17 +325,18 @@
 
     def pair(g):
         c_pack(g).wait_recv()
-        both = plus(packs[g, 0], packs[g, 1]).astype(BF)
-        pairs[g, zlo, 0] = both[:own // 2]
-        pairs[g, zlo, 1] = both[own // 2:]
-        for i in range(2):
-            c_pair(g, i).start()
+        pairs[g, zlo] = plus(packs[g, 0, core], packs[g, 1, core]).astype(BF)
+        c_pair(g).start()
+
+    def share(g):
+        c_pair(g).wait_recv()
+        totals[g, core] = plus(pairs[g, 0], pairs[g, 1])
+        c_share(g).start()
 
     def outer(g):
-        for i in range(2):
-            c_pair(g, i).wait_recv()
+        c_share(g).wait_recv()
         at = cols(g)
-        total = jnp.concatenate([plus(pairs[g, 0, i], pairs[g, 1, i]) for i in range(2)], axis=0)
+        total = jnp.concatenate([totals[g, 0], totals[g, 1]], axis=0)
         step = (jnp.exp2(powers(g)) * total) / REPS
         momentum = 0.9 * mom_v[:, at] + step
         mo_v[:, at] = momentum
@@ -340,8 +348,7 @@
         wide.drain(g)
         c_z(g).wait_send()
         c_pack(g).wait_send()
-        for i in range(2):
-            c_pair(g, i).wait_send()
+        c_pair(g).wait_send()
 
     def tidy_last(g):
         thin.drain(0)
@@ -349,17 +356,16 @@
             for rx in range(RING):
                 c_zx(ry, rx).wait_send()
         c_pack(g).wait_send()
-        for i in range(2):
-            c_pair(g, i).wait_send()
+        c_pair(g).wait_send()
 
     before = last - 1
     ends = dict(
         forward=lambda: wide.forward2(before), sum=lambda: second_sum(before), inner=lambda: inner(before),
-        pair=lambda: pair(before), outer=lambda: outer(before), tidy=lambda: tidy(before),
-        inner_last=lambda: inner_last(last), pair_last=lambda: pair(last), outer_last=lambda: outer(last),
+        pair=lambda: pair(before), share=lambda: share(before), outer=lambda: outer(before), tidy=lambda: tidy(before),
+        inner_last=lambda: inner_last(last), pair_last=lambda: pair(last), share_last=lambda: share(last), outer_last=lambda: outer(last),
         tidy_last=lambda: tidy_last(last))
 
-    everyone = [xp, xm, x2, yp, ym, y2, zdev, mate, *across]
+    everyone = [xp, xm, x2, yp, ym, y2, zdev, mate, across]
     barrier = pltpu.get_barrier_semaphore()
     for to in everyone:
         pl.semaphore_signal(barrier, inc=1, device_id=to, device_id_type=MESH)
@@ -415,7 +421,7 @@
             at_step(g, k, FLEADS[1], thin_forward, is_last)
             at_step(g, k, 0, wide.first_sum, is_wide)
             at_step(g, k, 0, thin_first_sum, is_last)
-            for lag, stage in zip(LAGS, (wide.forward2, second_sum, inner, pair, outer, tidy)):
+            for lag, stage in zip(LAGS, (wide.forward2, second_sum, inner, pair, share, outer, tidy)):
                 at_step(g, k, -lag, stage, is_early, "late")
             for step, stage in END:
                 if step % RING == k:
@@ -425,6 +431,7 @@
 
 
     for g in range(groups):
+        c_share(g).wait_send()
         for copy in inner_outs(g) + outer_outs(g):
             copy.wait()
 
@@ -489,7 +496,7 @@
             buf(*exponents.shape[::-1], kind=jnp.int32),
             buf(2, groups - 1, own, GW), buf(groups - 1, own, GW),
             buf(RING, RING, 2, own, GW), buf(RING, RING, own, GW),
-            buf(groups, 2, own, GW), buf(groups, 2, 2, own // 2, GW),
+            buf(groups, 2, 2, own // 2, GW), buf(groups, 2, own // 2, GW), buf(groups, 2, own // 2, GW, kind=F32),
             dma((RING * RING,)), dma((groups,)), dma((6,)), dma((5, groups)),
             dma((groups - 1,)), dma((groups - 1,)), dma((RING, RING)), dma((RING, RING)),
             dma((groups, 3)), dma((groups, 3)),

time: 83.9 us -> 83.8 us (level)
  no operation moved by 1% of the time
where the time goes in v5:
time: 83.8 us; the launch traced here: 83.6 us
  Pallas kernels  83 us (99%)
    pallas_call x1, Pallas kernels, local(): pl.pallas_call(kernel, out_shape=(jax.ShapeDtypeStruct(weight.shape, BF),...  80.4 us
    pallas_call x1, Pallas kernels, local(): pl.pallas_call(finish, out_shape=[jax.ShapeDtypeStruct(o.shape, o.dtype)...  2.58 us

profile of v5, /device:TPU:1, one launch (start us, length us, event | category | flops | bytes accessed | tf_op | source)
XLA Modules:
  0.0 83.6 jit_solution(17870437295809991754)
XLA Ops:
  0.6 80.4 %diloco_step.1 = (bf16[1,192,1024]{2,1,0:T(8,128)(2,1)}, bf16[1,192,1024]{2,1,0:T(8,128)(2,1)}, bf16[1,192,1024]{2,1,0:T(8,128)(2,1)}, bf16[192,1024]{1,0:T(8,128)(2,1)}, f32[192,1024]{1,0:T(8,128)}) custom-call(bf16[1,512,6144]{2,1,0:T(8,128)(2,1)} %act.1, bf16[1,512,1024]{2,1,0:T(8,128)(2,1)} %cot.1, bf16[1,192,1024]{2,1,0:T(8,128)(2,1)} %weight.1, ...), custom_call_target="tpu_custom_call" | custom-call | flops 6442450944 | bytes 12582912 | tf_op jit(solution)/shard_map/diloco_step/pallas_call | solution.py:481
  81.0 2.6 %results.1 = (bf16[1,192,1024]{2,1,0:T(8,128)(2,1)}, bf16[1,192,1024]{2,1,0:T(8,128)(2,1)}, bf16[1,192,1024]{2,1,0:T(8,128)(2,1)}, bf16[192,1024]{1,0:T(8,128)(2,1)}, f32[192,1024]{1,0:T(8,128)}) custom-call(bf16[1,192,1024]{2,1,0:T(8,128)(2,1)} %get-tuple-element.10.refs_0_, bf16[1,192,1024]{2,1,0:T(8,128)(2,1)} %get-tuple-element.11.refs_1_, ...), custom_call_target="tpu_custom_call" | custom-call | tf_op jit(solution)/shard_map/results/pallas_call | solution.py:510

commit v6 on v5

--- a/solution.py
+++ b/solution.py
@@ -237,11 +237,15 @@
         return lax.dot_general(
             a_v[:, at], c_v[:, cols(g)], (((0,), (0,)), ((), ())), preferred_element_type=F32).astype(BF)
 
-    def products(g, k):
-        @pl.when(g == 0)
-        def _():
+    def products(g, k, first=False):
+        if first:
             for ry, rx in NEW_BLOCKS[k]:
                 a_copy(((y + OFFS[ry]) % RING) * RING + (x + OFFS[rx]) % RING).wait()
+        elif k > 0:
+            @pl.when(g == 0)
+            def _():
+                for ry, rx in NEW_BLOCKS[k]:
+                    a_copy(((y + OFFS[ry]) % RING) * RING + (x + OFFS[rx]) % RING).wait()
 
         if k == 0:
             c_copy(g).wait()
@@ -249,15 +253,9 @@
             wide.place(g, ry, rx, product(g, ry, rx))
             for h in range(2):
                 if n + 1 == SEND_AFTER[k][h]:
-                    if k == 0 and h == 0:
-                        @pl.when(g == 0)
-                        def _():
-                            pl.semaphore_wait(barrier, len(everyone))
+                    if first and h == 0:
+                        pl.semaphore_wait(barrier, len(everyone))
                     wide.send(h, g, k)
-        if k == 0:
-            @pl.when(g == 0)
-            def _():
-                load_rest()
 
     def exchange(n):
         if n == 0:
@@ -384,11 +382,13 @@
 
     c_copy(0).start()
     load(0)
-
-    def at_step(g, k, shift, stage, groups_of, *late):
+    products(0, 0, first=True)
+    load_rest()
+
+    def at_step(g, k, shift, stage, groups_of, *late, after=0):
         group, kk = g + (k + shift) // RING, (k + shift) % RING
         if not late or kk == RING - 1:
-            @pl.when(groups_of(group))
+            @pl.when(jnp.logical_and(groups_of(group), group * RING + kk >= after))
             def _():
                 stage(group) if late else stage(group, kk)
 
@@ -408,7 +408,9 @@
     def _(turn):
         g = turn + first_turn
         for k in range(RING):
-            at_step(g, k, LEADS[0], products, is_wide)
+            at_step(g, k, FLEADS[0], wide.forward, is_wide)
+            at_step(g, k, FLEADS[1], thin_forward, is_last)
+            at_step(g, k, LEADS[0], products, is_wide, after=1)
             at_step(g, k, LEADS[1], products_last, is_last)
             for n in range(len(BATCHES)):
                 step = n + EXCHANGE
@@ -416,9 +418,6 @@
                     @pl.when(g == step // RING)
                     def _():
                         exchange(n)
-
-            at_step(g, k, FLEADS[0], wide.forward, is_wide)
-            at_step(g, k, FLEADS[1], thin_forward, is_last)
             at_step(g, k, 0, wide.first_sum, is_wide)
             at_step(g, k, 0, thin_first_sum, is_last)
             for lag, stage in zip(LAGS, (wide.forward2, second_sum, inner, pair, share, outer, tidy)):

time: 83.8 us -> 84 us (level)
  no operation moved by 1% of the time
where the time goes in v6:
time: 84 us; the launch traced here: 83.8 us
  Pallas kernels  83.1 us (99%)
    pallas_call x1, Pallas kernels, local(): pl.pallas_call(kernel, out_shape=(jax.ShapeDtypeStruct(weight.shape, BF),...  80.6 us
    pallas_call x1, Pallas kernels, local(): pl.pallas_call(finish, out_shape=[jax.ShapeDtypeStruct(o.shape, o.dtype)...  2.58 us

profile of v6, /device:TPU:1, one launch (start us, length us, event | category | flops | bytes accessed | tf_op | source)
XLA Modules:
  0.0 83.8 jit_solution(4618989647044279959)
XLA Ops:
  0.6 80.6 %diloco_step.1 = (bf16[1,192,1024]{2,1,0:T(8,128)(2,1)}, bf16[1,192,1024]{2,1,0:T(8,128)(2,1)}, bf16[1,192,1024]{2,1,0:T(8,128)(2,1)}, bf16[192,1024]{1,0:T(8,128)(2,1)}, f32[192,1024]{1,0:T(8,128)}) custom-call(bf16[1,512,6144]{2,1,0:T(8,128)(2,1)} %act.1, bf16[1,512,1024]{2,1,0:T(8,128)(2,1)} %cot.1, bf16[1,192,1024]{2,1,0:T(8,128)(2,1)} %weight.1, ...), custom_call_target="tpu_custom_call" | custom-call | flops 6442450944 | bytes 12582912 | tf_op jit(solution)/shard_map/diloco_step/pallas_call | solution.py:480
  81.2 2.6 %results.1 = (bf16[1,192,1024]{2,1,0:T(8,128)(2,1)}, bf16[1,192,1024]{2,1,0:T(8,128)(2,1)}, bf16[1,192,1024]{2,1,0:T(8,128)(2,1)}, bf16[192,1024]{1,0:T(8,128)(2,1)}, f32[192,1024]{1,0:T(8,128)}) custom-call(bf16[1,192,1024]{2,1,0:T(8,128)(2,1)} %get-tuple-element.10.refs_0_, bf16[1,192,1024]{2,1,0:T(8,128)(2,1)} %get-tuple-element.11.refs_1_, ...), custom_call_target="tpu_custom_call" | custom-call | tf_op jit(solution)/shard_map/results/pallas_call | solution.py:509
